TPU v7x, 256 devices: a whole 4x4x8 slice. The times are simulated.
256 devices in a mesh: pair: 2 (over x_hi), tp: 8 (over y, x_lo), dp: 16 (over z, core).
Axes of the slice: x: 4 (x_hi: 2, x_lo: 2; x = x_hi * 2 + x_lo), y: 4, z: 8, core: 2. Of those that a mesh axis runs over, the one named last changes fastest.
Arguments:
- x_prompt: bfloat16 [16, 512, 4608], P('dp', ('pair', 'tp')), may hold values from -6 to 6
- x_comp: bfloat16 [16, 2, 128, 4608], P('dp', 'pair', 'tp'), may hold values from -6 to 6
- up_prompt: bfloat16 [16, 512, 4608], P('dp', ('pair', 'tp')), may hold values from -0.4 to 0.4
- up_comp: bfloat16 [16, 2, 128, 4608], P('dp', 'pair', 'tp'), may hold values from -0.4 to 0.4
- w_q: bfloat16 [4608, 2048], P(None, 'tp'), may hold values from -0.14731391 to 0.14731391
- key_projection: bfloat16 [4608, 1024], P(None, 'tp'), may hold values from -0.09375 to 0.09375
- value_projection: bfloat16 [4608, 1024], P(None, 'tp'), may hold values from -0.09375 to 0.09375
- w_o: bfloat16 [2048, 4608], P('tp'), may hold values from -0.15467961 to 0.15467961
- pre_gain: float32 [4608], replicated, may hold values from 0.5 to 1.5
- post_gain: float32 [4608], replicated, may hold values from 0.25 to 1.75
- dpo_weight: float32 [16], P('dp'), may hold values from 0.1 to 1
- prompt_len: int32 [16], P('dp'), may hold values from 257 to 512, as said below
- comp_len: int32 [16, 2], P('dp', 'pair'), may hold values from 32 to 128, as said below
- loss_mask: int32 [16, 2, 128], P('dp', 'pair'), may hold values 0 or 1
Outputs:
- out_prompt: bfloat16 [16, 512, 4608], P('dp', ('pair', 'tp'))
- out_comp: bfloat16 [16, 2, 128, 4608], P('dp', 'pair', 'tp')
- grad_wq: float32 [4608, 2048], P(('pair', 'dp'), 'tp')
- grad_wk: float32 [4608, 1024], P(('pair', 'dp'), 'tp')
- grad_wv: float32 [4608, 1024], P(('pair', 'dp'), 'tp')
- grad_wo: float32 [2048, 4608], P('tp', ('pair', 'dp'))
Inputs may be any that keep to these rules, and one draw needn't show every extreme that they name: Tokens past prompt_len are padding; some pair's prompt has all 512 tokens real. Tokens past comp_len are padding; some completion has all 128 tokens real.
All inputs are finite; a program needn't handle non-finite values. No bound on the sum of `loss_mask` on one device may be relied on, other than what follows from the above.
Results may differ from a plain program's by a relative error of at most 0.029.
Values may be sent and summed in bfloat16 or wider, within the bound.
A program may use at most 128 MiB of HBM per device.

v0:
```python
import jax
import numpy as np
import jax.numpy as jnp
from jax import lax
from jax.experimental import pallas as pl
from jax.experimental.pallas import tpu as pltpu
from jax.sharding import PartitionSpec as P

HEAD_SIZE = 128


softcap = 50.0
query_scale = 144.0 ** (-0.5)
rope_base = 10000.0
norm_eps = 1e-06


MESH = pl.DeviceIdType.MESH
PIECE = 768
PLUS, MINUS, CROSS = 0, 1, 2
STEPS = 14
SENDS = (
    [
        ((0, 0), 5),
        ((0, 0), 0),
        ((0, 0), 3),
        ((0, 0), 2),
        ((0, 0), 4),
        ((0, 0), 1),
        ((1, 0), 3),
        ((0, -1), 3),
        ((1, 0), 4),
        ((0, -1), 4),
        ((0, -1), 5),
        ((1, -1), 3),
        ((1, -1), 5),
        ((1, -1), 4),
    ],
    [
        ((0, 0), 2),
        ((0, 0), 1),
        ((0, 0), 0),
        ((0, 0), 4),
        ((0, 0), 3),
        ((0, 0), 5),
        ((1, 0), 0),
        ((0, 1), 1),
        ((1, 0), 1),
        ((0, 1), 2),
        ((0, 1), 0),
        ((1, 1), 0),
        ((1, 1), 2),
        ((1, 1), 1),
    ],
    [
        ((0, 0), 3),
        ((0, 0), 0),
        ((0, 0), 4),
        ((0, 0), 1),
        ((0, 0), 5),
        ((0, 1), 2),
        ((0, -1), 5),
        ((0, -1), 0),
        ((0, 0), 2),
        ((0, -1), 2),
        ((0, -1), 1),
        ((0, 1), 5),
        ((0, 1), 3),
        ((0, 1), 4),
    ],
)


def seen_from(stream, owner):
    flip, shift = owner
    if stream == CROSS:
        return (1 - flip, shift % 4)
    return (flip, (shift + (1 if stream == MINUS else -1)) % 4)


ARRIVALS = tuple(
    [(seen_from(s, owner), piece) for owner, piece in SENDS[s]] for s in range(3)
)


def ready_step(stream, pos):
    (flip, shift), piece = SENDS[stream][pos]
    if (flip, shift) == (0, 0):
        return -1
    spots = [
        p
        for s in range(3)
        for p in range(STEPS)
        if ARRIVALS[s][p] == ((flip, shift % 4), piece)
    ]
    return spots[0]


def tp_rank_of(owner):
    me = lax.axis_index("tp")
    flip, shift = owner
    return lax.rem(me // 2 + shift % 4, 4) * 2 + lax.rem(me + flip, 2)


def stream_target(stream):
    return {"tp": tp_rank_of([(0, 1), (0, 3), (1, 0)][stream])}


def stream_source(stream):
    return {"tp": tp_rank_of([(0, 3), (0, 1), (1, 0)][stream])}


def tp_barrier():
    barrier = pltpu.get_barrier_semaphore()
    for stream in range(3):
        pl.semaphore_signal(
            barrier, inc=1, device_id=stream_target(stream), device_id_type=MESH
        )
    pl.semaphore_wait(barrier, 3)


def cols(piece):
    return pl.ds(piece * PIECE, PIECE)


def wait_all_sends(comm):
    blocks = comm.buf.at[pl.ds(0, 7), comm.rows]
    pltpu.make_async_remote_copy(
        src_ref=blocks,
        dst_ref=blocks,
        send_sem=comm.send_sems.at[comm.first // (3 * STEPS)],
        recv_sem=comm.recv_sems.at[comm.first],
        device_id=stream_target(CROSS),
        device_id_type=MESH,
    ).wait_send()


class Gather:
    def __init__(self, buf, rows, send_sems, recv_sems, first_sem=0):
        self.buf, self.rows = buf, rows
        self.send_sems, self.recv_sems, self.first = send_sems, recv_sems, first_sem
        self.started = [0, 0, 0]

    def copy(self, stream, pos):
        owner, piece = SENDS[stream][pos]
        ref = self.buf.at[tp_rank_of(owner), self.rows, cols(piece)]
        sem = self.first + stream * STEPS + pos
        return pltpu.make_async_remote_copy(
            src_ref=ref,
            dst_ref=ref,
            send_sem=self.send_sems.at[self.first // (3 * STEPS)],
            recv_sem=self.recv_sems.at[sem],
            device_id=stream_target(stream),
            device_id_type=MESH,
        )

    def arrival(self, stream, pos):
        owner, piece = ARRIVALS[stream][pos]
        ref = self.buf.at[tp_rank_of(owner), self.rows, cols(piece)]
        sem = self.first + stream * STEPS + pos
        return pltpu.make_async_remote_copy(
            src_ref=ref,
            dst_ref=ref,
            send_sem=self.send_sems.at[self.first // (3 * STEPS)],
            recv_sem=self.recv_sems.at[sem],
            device_id=stream_target(stream),
            device_id_type=MESH,
        )

    def push(self, arrived):
        for pos in range(STEPS):
            for stream in range(3):
                if pos == self.started[stream] and ready_step(stream, pos) <= arrived:
                    self.copy(stream, pos).start()
                    self.started[stream] += 1

    def start(self):
        self.push(-1)

    def step(self, t):
        for stream in range(3):
            self.arrival(stream, t).wait_recv()
        self.push(t)

    def finish_sends(self):
        wait_all_sends(self)


def needed_step(stream, back):
    owner, piece = ARRIVALS[stream][STEPS - 1 - back]
    spots = [
        STEPS - 1 - p
        for s in range(3)
        for p in range(STEPS)
        if ((SENDS[s][p][0][0], SENDS[s][p][0][1] % 4), SENDS[s][p][1]) == (owner, piece)
    ]
    return max(spots, default=-1)


class Reduce:
    def __init__(self, buf, rows, got, send_sems, recv_sems, first_sem=0):
        self.buf, self.rows, self.got = buf, rows, got
        self.send_sems, self.recv_sems, self.first = send_sems, recv_sems, first_sem
        self.started = [0, 0, 0]

    def copy(self, stream, back):
        owner, piece = ARRIVALS[stream][STEPS - 1 - back]
        sem = self.first + stream * STEPS + back
        return pltpu.make_async_remote_copy(
            src_ref=self.buf.at[tp_rank_of(owner), self.rows, cols(piece)],
            dst_ref=self.got.at[stream * STEPS + back, self.rows],
            send_sem=self.send_sems.at[self.first // (3 * STEPS)],
            recv_sem=self.recv_sems.at[sem],
            device_id=stream_source(stream),
            device_id_type=MESH,
        )

    def push(self, arrived):
        for back in range(STEPS):
            for stream in range(3):
                if back == self.started[stream] and needed_step(stream, back) <= arrived:
                    self.copy(stream, back).start()
                    self.started[stream] += 1

    def start(self):
        self.push(-1)

    def step(self, t):
        for stream in range(3):
            self.copy(stream, t).wait_recv()
            owner, piece = SENDS[stream][STEPS - 1 - t]
            rank = tp_rank_of(owner)
            self.buf[rank, self.rows, cols(piece)] = (
                self.buf[rank, self.rows, cols(piece)].astype(jnp.float32)
                + self.got[stream * STEPS + t, self.rows].astype(jnp.float32)
            ).astype(jnp.bfloat16)
        self.push(t)

    def finish_sends(self):
        wait_all_sends(self)


class Ticker:
    def __init__(self):
        self.todo = []

    def add(self, steps):
        self.todo += steps

    def tick(self, count=1):
        for _ in range(count):
            if self.todo:
                self.todo.pop(0)()

    def drain(self):
        self.tick(len(self.todo))


def nt_dot(a, b):
    return lax.dot_general(a, b, (((1,), (1,)), ((), ())), preferred_element_type=jnp.float32)


def tn_dot(a, b):
    return lax.dot_general(a, b, (((0,), (0,)), ((), ())), preferred_element_type=jnp.float32)


def nn_dot(a, b):
    return jnp.dot(a, b, preferred_element_type=jnp.float32)


def turn(values, cosine, sine):
    return values * cosine + pltpu.roll(values, HEAD_SIZE // 2, 1) * sine


def inverse_norm(values):
    return lax.rsqrt(jnp.mean(values * values, axis=-1, keepdims=True) + norm_eps)


def iota(shape, dim):
    return lax.broadcasted_iota(jnp.int32, shape, dim)


def block_kernel(
    x_p, x_c, up_p, up_c, w_q, w_k, w_v, w_o, pre_gain, post_gain,
    rope, dpo_weight, prompt_len, comp_len, loss_mask,
    out_p, out_c, grad_wq, grad_wk, grad_wv, grad_wo,
    cos_p, sin_p, cos_c, sin_c, table, xp, xc, upp, upc, wqkv, wo, nbp, nbc, brp, brc, gotp, gotc, gbp, gbc,
    qs, kv, att, prob_p, prob_c, damp_p, damp_c, dkv, dkv_out, dkv_in, gq, gkv,
    wg, core_in, a_half, a_full, b_up, b_down, b_full, pair_out, pair_in, cross_out, cross_in,
    load_sems, tp_send, tp_recv, kv_send, kv_recv, core_send, core_recv,
    z_send, z_recv, pair_send, pair_recv, cross_send, cross_recv,
):
    side = lax.axis_index("pair")
    me = lax.axis_index("tp")
    dp = lax.axis_index("dp")
    core, z = lax.rem(dp, 2), dp // 2
    partner = {"pair": 1 - side}
    other_core = {"dp": dp + 1 - 2 * core}
    z_up, z_down = {"dp": lax.rem(dp + 2, 16)}, {"dp": lax.rem(dp + 14, 16)}
    rows_p, rows_c = xp.shape[0], xc.shape[0]
    half, comp = 8 * rows_p, 8 * rows_c
    prompt = 2 * half
    width = xp.shape[1]
    pieces = width // PIECE

    loads = [
        pltpu.make_async_copy(source, target, load_sems.at[i])
        for i, (source, target) in enumerate(
            [
                (x_p, xp), (x_c, xc),
                (w_q, wqkv.at[:, 0:256]), (w_k, wqkv.at[:, 256:384]), (w_v, wqkv.at[:, 384:512]),
                (w_o, wo), (up_p, upp), (up_c, upc), (rope, table),
            ]
        )
    ]
    for load in loads:
        load.start()
    barrier = pltpu.get_barrier_semaphore()
    peers = [stream_target(s) for s in range(3)] + [partner, other_core, z_up, z_down]
    for peer in peers:
        pl.semaphore_signal(barrier, inc=1, device_id=peer, device_id_type=MESH)

    gain_in = pre_gain[...].reshape(1, width)
    gain_out = post_gain[...].reshape(1, width)

    def normalize(x):
        values = x[...].astype(jnp.float32)
        return (values * inverse_norm(values) * gain_in).astype(jnp.bfloat16)

    all_p, all_c = pl.ds(0, rows_p), pl.ds(0, rows_c)
    n = 3 * STEPS
    gather_p = Gather(nbp, all_p, tp_send, tp_recv, 0)
    gather_c = Gather(nbc, all_c, tp_send, tp_recv, n)
    reduce_p = Reduce(brp, all_p, gotp, tp_send, tp_recv, 2 * n)
    reduce_c = Reduce(brc, all_c, gotc, tp_send, tp_recv, 3 * n)
    regather_p = Gather(gbp, all_p, tp_send, tp_recv, 4 * n)
    regather_c = Gather(gbc, all_c, tp_send, tp_recv, 5 * n)
    ticker = Ticker()
    tick = ticker.tick

    def steps_of(comm):
        return [lambda t=t: comm.step(t) for t in range(STEPS)]

    loads[0].wait()
    nbp[me] = normalize(xp)
    pl.semaphore_wait(barrier, len(peers))
    gather_p.start()
    loads[1].wait()
    nbc[me] = normalize(xc)
    for t in range(STEPS):
        gather_p.step(t)
        if t == 10:
            gather_c.start()
    ticker.add(steps_of(gather_c))
    for load in loads[2:5]:
        load.wait()

    def project(buf, count, every):
        total = jnp.zeros((count, 512), jnp.float32)
        for k in range(pieces):
            total += nn_dot(
                buf[:, :, k * PIECE : (k + 1) * PIECE].reshape(count, PIECE),
                wqkv[k * PIECE : (k + 1) * PIECE],
            )
            tick(every)
        return total

    def place(total, cosine, sine, first, key_first, count):
        for h in range(2):
            here = slice(h * 128, (h + 1) * 128)
            qs[first : first + count, here] = (
                turn(total[:, here], cosine[...], sine[...]) * query_scale
            ).astype(jnp.bfloat16)
        kv[key_first : key_first + count, 0:128] = turn(
            total[:, 256:384], cosine[...], sine[...]
        ).astype(jnp.bfloat16)
        kv[key_first : key_first + count, 128:256] = total[:, 384:512].astype(jnp.bfloat16)

    loads[8].wait()
    length = prompt_len[0]

    def spread(packed, cosine, sine):
        swapped = pltpu.roll(packed, HEAD_SIZE // 2, 1)
        low = iota(packed.shape, 1) < HEAD_SIZE // 2
        cosine[...] = jnp.where(low, packed, swapped)
        sine[...] = jnp.where(low, -swapped, packed)

    spread(table[pl.ds(pl.multiple_of(side * half, half), half), :], cos_p, sin_p)
    spread(table[pl.ds(length, comp), :], cos_c, sin_c)
    place(project(nbp, half, 1), cos_p, sin_p, 0, 0, half)
    kv_copy = pltpu.make_async_remote_copy(
        src_ref=kv.at[pl.ds(0, half)],
        dst_ref=kv.at[pl.ds(half, half)],
        send_sem=kv_send.at[0],
        recv_sem=kv_recv.at[0],
        device_id=partner,
        device_id_type=MESH,
    )
    kv_copy.start()
    loads[5].wait()
    tick(4)

    def attend(h, first, count, keys, allowed, prob, damp):
        here = slice(h * 128, (h + 1) * 128)
        scores = nt_dot(qs[first : first + count, here], kv[0:keys, 0:128])
        bounded = jnp.tanh(scores / softcap)
        raw = jnp.where(allowed, jnp.exp(softcap * bounded), 0.0)
        probs = raw / jnp.sum(raw, axis=-1, keepdims=True)
        prob[h] = probs
        damp[h] = 1.0 - bounded * bounded
        att[first : first + count, here] = nn_dot(
            probs.astype(jnp.bfloat16), kv[0:keys, 128:256]
        ).astype(jnp.bfloat16)

    def project_out(first, count, buf, every):
        for k in range(pieces):
            here = slice(k * PIECE, (k + 1) * PIECE)
            term = nn_dot(att[first : first + count, :], wo[:, here]).astype(jnp.bfloat16)
            buf[:, :, here] = term.reshape(8, count // 8, PIECE)
            tick(every)

    row, col = iota((half, prompt), 0), iota((half, prompt), 1)
    allowed_p = ((col < half) & (col <= row)) | ((col >= half) & (side == 1))
    kv_copy.wait_recv()
    for h in range(2):
        attend(h, 0, half, prompt, allowed_p, prob_p, damp_p)
        tick(1)
    project_out(0, half, brp, 0)
    reduce_p.start()
    ticker.drain()
    ticker.add(steps_of(reduce_p))
    place(project(nbc, comp, 0), cos_c, sin_c, half, prompt, comp)
    tick(1)

    row, col = iota((comp, prompt + comp), 0), iota((comp, prompt + comp), 1)
    token = jnp.where(col < half, col + side * half, col - half + (1 - side) * half)
    allowed_c = ((col < prompt) & (token < length)) | ((col >= prompt) & (col - prompt <= row))
    for h in range(2):
        attend(h, half, comp, prompt + comp, allowed_c, prob_c, damp_c)
        tick(2)
    project_out(half, comp, brc, 1)
    tick(1)
    reduce_c.start()
    gather_p.finish_sends()
    gather_c.finish_sends()
    ticker.drain()

    def finish_branch(x, up, branch_rows, factor):
        branch = branch_rows.astype(jnp.float32)
        scale = inverse_norm(branch)
        out = (x[...].astype(jnp.float32) + branch * scale * gain_out).astype(jnp.bfloat16)
        scaled = up[...].astype(jnp.float32) * factor * gain_out
        inner = jnp.mean(branch * scaled, axis=-1, keepdims=True)
        grad = (scale * scaled - branch * (scale * scale * scale) * inner).astype(jnp.bfloat16)
        return out, grad

    loads[6].wait()
    loads[7].wait()
    token = side * half + me * rows_p + iota((rows_p, 1), 0)
    out_p[...], gbp[me] = finish_branch(xp, upp, brp[me], (token < length).astype(jnp.float32))
    regather_p.start()
    ticker.add(steps_of(reduce_c))
    ticker.drain()
    slot = iota((rows_c, 1), 0)
    keep = jnp.zeros((rows_c, 1), jnp.float32)
    for i in range(rows_c):
        keep = jnp.where(slot == i, loss_mask[me * rows_c + i].astype(jnp.float32), keep)
    direction = 1.0 - 2.0 * side.astype(jnp.float32)
    real = (me * rows_c + slot < comp_len[0, 0]).astype(jnp.float32)
    out_c[...], gbc[me] = finish_branch(
        xc, upc, brc[me], dpo_weight[0] * direction * keep * real
    )
    for t in range(STEPS):
        regather_p.step(t)
        if t == 10:
            regather_c.start()
            reduce_p.finish_sends()
            reduce_c.finish_sends()
    ticker.add(steps_of(regather_c))

    def grad_of_attended(buf, count, every):
        total = jnp.zeros((count, 256), jnp.float32)
        for k in range(pieces):
            here = slice(k * PIECE, (k + 1) * PIECE)
            total += nt_dot(buf[:, :, here].reshape(count, PIECE), wo[:, here])
            tick(every)
        return total.astype(jnp.bfloat16)

    def attend_back(h, grad, first, count, keys, prob, damp, cosine, sine):
        here = slice(h * 128, (h + 1) * 128)
        grad_h = grad[:, here]
        grad_probs = nt_dot(grad_h, kv[0:keys, 128:256])
        probs = prob[h]
        value_part = tn_dot(probs.astype(jnp.bfloat16), grad_h)
        centered = probs * (grad_probs - jnp.sum(probs * grad_probs, axis=-1, keepdims=True))
        grad_scores = (centered * damp[h]).astype(jnp.bfloat16)
        grad_q = nn_dot(grad_scores, kv[0:keys, 0:128])
        key_part = tn_dot(grad_scores, qs[first : first + count, here])
        gq[first : first + count, here] = (
            turn(grad_q, cosine[...], -sine[...]) * query_scale
        ).astype(jnp.bfloat16)
        return key_part, value_part

    grad = grad_of_attended(gbp, half, 1)
    key_0, value_0 = attend_back(0, grad, 0, half, prompt, prob_p, damp_p, cos_p, sin_p)
    tick(3)
    key_1, value_1 = attend_back(1, grad, 0, half, prompt, prob_p, damp_p, cos_p, sin_p)
    dkv[0:prompt, 0:128] = key_0 + key_1
    dkv[0:prompt, 128:256] = value_0 + value_1
    ticker.drain()

    def remote(src, dst, send_sem, recv_sem, device):
        return pltpu.make_async_remote_copy(
            src_ref=src, dst_ref=dst, send_sem=send_sem, recv_sem=recv_sem,
            device_id=device, device_id_type=MESH,
        )

    sent = []

    def start(copy):
        copy.start()
        sent.append(copy)

    def at_z(shift):
        return lax.rem(z + shift, 8)

    def chunk_side(j):
        return 1 - side if j < 2 else side

    def core_copy(third, j):
        spot = (third, slice(None), chunk_side(j), pl.ds((j % 2) * 4, 4))
        return remote(
            wg.at[spot + (1 - core,)], core_in.at[spot],
            core_send.at[third * 4 + j], core_recv.at[third * 4 + j], other_core,
        )

    def weight_terms(third, left_p, left_c, right_p, right_c):
        per = 1152
        for j in range(width // per):
            here = pl.ds(pl.multiple_of((chunk_side(j) * 2 + j % 2) * per, per), per)
            term = tn_dot(left_p[:, :, here].reshape(half, per), right_p) + tn_dot(
                left_c[:, :, here].reshape(comp, per), right_c
            )
            term = term.astype(jnp.bfloat16)
            for way in range(2):
                wg[third, way, chunk_side(j), (j % 2) * 4 : (j % 2) * 4 + 4] = (
                    term[:, way * 128 : (way + 1) * 128].reshape(4, 2, 144, 128)
                )
            start(core_copy(third, j))

    def core_sum(third, way, p, at):
        return wg[third, way, p, at, core].astype(jnp.float32) + core_in[
            third, way, p, at
        ].astype(jnp.float32)

    def keep(third, way, p, at, value):
        wg[third, way, p, at, core] = value.astype(jnp.bfloat16)

    CROSS_ORDER = (4, 3, 5, 2, 6, 1, 7, 0)

    CROSS_PARTS = ((0, 3), (3, 5))

    def cross_copy(third, part):
        blocks = pl.ds(*CROSS_PARTS[part])
        return remote(
            cross_out.at[third, blocks], cross_in.at[third, blocks],
            cross_send.at[third * 2 + part], cross_recv.at[third * 2 + part], partner,
        )

    def b_sum(third, shift):
        i = CROSS_ORDER.index(shift)
        for part in range(2):
            if i == CROSS_PARTS[part][0]:
                cross_copy(third, part).wait_recv()
        return core_sum(third, 1, side, at_z(shift)) + cross_in[third, i].astype(jnp.float32)

    def z_copy(third, way, step, upward):
        shift = (4 - step) if upward else (4 + step)
        at = at_z(shift)
        to = 0 if upward else 1
        if way == 0 and step == 0:
            block, target = wg.at[third, 0, to, at, core], a_half.at[third, to]
        elif way == 0:
            block, target = wg.at[third, 0, :, at, core], a_full.at[third, to, step - 1]
        elif step == 0:
            rows = pl.ds(0, 80) if upward else pl.ds(80, 64)
            block = wg.at[third, 1, side, at, core, rows]
            target = (b_up if upward else b_down).at[third]
        else:
            block = wg.at[third, 1, side, at, core]
            target = b_full.at[third, to, step - 1]
        sem = (third * 2 + way) * 8 + step * 2 + to
        return remote(
            block, target, z_send.at[sem], z_recv.at[sem], z_up if upward else z_down
        )

    def z_start(third, way):
        if way == 0:
            for p in range(2):
                keep(third, 0, p, at_z(4), core_sum(third, 0, p, at_z(4)))
        else:
            keep(third, 1, side, at_z(4), b_sum(third, 4))
        start(z_copy(third, way, 0, True))
        start(z_copy(third, way, 0, False))

    def z_step(third, way, step):
        for upward in (True, False):
            shift = (3 - step) if upward else (5 + step)
            at = at_z(shift)
            to = 0 if upward else 1
            if way == 0:
                z_copy(third, 0, step, upward).wait_recv()
                for p in range(2):
                    value = core_sum(third, 0, p, at)
                    if step > 0:
                        value += a_full[third, to, step - 1, p].astype(jnp.float32)
                    elif p == to:
                        value += a_half[third, to].astype(jnp.float32)
                    keep(third, 0, p, at, value)
            else:
                value = b_sum(third, shift)
                z_copy(third, 1, step, upward).wait_recv()
                if step == 0 and upward:
                    arrived = jnp.concatenate(
                        [b_up[third].astype(jnp.float32), jnp.zeros((64, 128), jnp.float32)], axis=0
                    )
                elif step == 0:
                    arrived = jnp.concatenate(
                        [jnp.zeros((80, 128), jnp.float32), b_down[third].astype(jnp.float32)],
                        axis=0,
                    )
                else:
                    arrived = b_full[third, to, step - 1].astype(jnp.float32)
                keep(third, 1, side, at, value + arrived)
            start(z_copy(third, way, step + 1, upward))

    def pair_copy(third):
        return remote(
            pair_out.at[third], pair_in.at[third],
            pair_send.at[third], pair_recv.at[third], partner,
        )

    def last_a(third):
        z_copy(third, 0, 3, True).wait_recv()
        z_copy(third, 0, 3, False).wait_recv()

        def total(p):
            return (
                core_sum(third, 0, p, z)
                + a_full[third, 0, 2, p].astype(jnp.float32)
                + a_full[third, 1, 2, p].astype(jnp.float32)
            )

        pair_out[third] = total(1 - side).astype(jnp.bfloat16)
        start(pair_copy(third))
        return total(side)

    def whole_a(third, own):
        pair_copy(third).wait_recv()
        return own + pair_in[third].astype(jnp.float32)

    def whole_b(third):
        value = b_sum(third, 0)
        z_copy(third, 1, 3, True).wait_recv()
        z_copy(third, 1, 3, False).wait_recv()
        return (
            value
            + b_full[third, 0, 2].astype(jnp.float32)
            + b_full[third, 1, 2].astype(jnp.float32)
        )

    def launch_b(third):
        for j in range(2):
            core_copy(third, j).wait_recv()
        for part, (first, count) in enumerate(CROSS_PARTS):
            for i in range(first, first + count):
                cross_out[third, i] = core_sum(third, 1, 1 - side, at_z(CROSS_ORDER[i])).astype(
                    jnp.bfloat16
                )
            start(cross_copy(third, part))

    def launch_a(third):
        for j in range(2, 4):
            core_copy(third, j).wait_recv()
        z_start(third, 0)

    def settle():
        for copy in sent:
            copy.wait_send()
        sent.clear()

    weight_terms(0, gbp, gbc, att[0:half, :], att[half : half + comp, :])
    grad = grad_of_attended(gbc, comp, 0)
    parts = [
        attend_back(h, grad, half, comp, prompt + comp, prob_c, damp_c, cos_c, sin_c)
        for h in range(2)
    ]
    dkv[0:prompt, 0:128] += parts[0][0][0:prompt] + parts[1][0][0:prompt]
    dkv[0:prompt, 128:256] += parts[0][1][0:prompt] + parts[1][1][0:prompt]
    dkv_out[...] = dkv[half:prompt, :].astype(jnp.bfloat16)
    dkv_copy = remote(dkv_out, dkv_in, kv_send.at[1], kv_recv.at[1], partner)
    start(dkv_copy)
    gkv[half : half + comp, 0:128] = turn(
        parts[0][0][prompt:] + parts[1][0][prompt:], cos_c[...], -sin_c[...]
    ).astype(jnp.bfloat16)
    gkv[half : half + comp, 128:256] = (parts[0][1][prompt:] + parts[1][1][prompt:]).astype(
        jnp.bfloat16
    )
    launch_b(0)
    weight_terms(1, nbp, nbc, gq[0:half, :], gq[half : half + comp, :])
    launch_a(0)
    launch_b(1)
    launch_a(1)
    z_step(0, 0, 0)
    dkv_copy.wait_recv()
    whole = dkv[0:half, :] + dkv_in[...].astype(jnp.float32)
    gkv[0:half, 0:128] = turn(whole[:, 0:128], cos_p[...], -sin_p[...]).astype(jnp.bfloat16)
    gkv[0:half, 128:256] = whole[:, 128:256].astype(jnp.bfloat16)
    weight_terms(2, nbp, nbc, gkv[0:half, :], gkv[half : half + comp, :])
    z_start(0, 1)
    z_step(1, 0, 0)
    launch_b(2)
    z_step(0, 0, 1)
    launch_a(2)
    z_start(1, 1)
    z_step(1, 0, 1)
    z_step(0, 1, 0)
    z_step(2, 0, 0)
    z_step(1, 1, 0)
    z_step(0, 0, 2)
    z_start(2, 1)
    z_step(2, 0, 1)
    z_step(1, 1, 1)
    z_step(2, 1, 0)
    kv_copy.wait_send()
    regather_p.finish_sends()
    regather_c.finish_sends()
    z_step(1, 0, 2)
    z_step(2, 0, 2)
    z_step(0, 1, 1)
    own_0 = last_a(0)
    z_step(2, 1, 1)
    z_step(1, 1, 2)
    own_2 = last_a(2)
    z_step(0, 1, 2)
    own_1 = last_a(1)
    settle()
    z_step(2, 1, 2)
    grad_wk[...] = whole_a(2, own_2)
    grad_wo[:, 128:256] = whole_b(0)
    grad_wo[:, 0:128] = whole_a(0, own_0)
    grad_wq[:, 0:128] = whole_a(1, own_1)
    grad_wq[:, 128:256] = whole_b(1)
    settle()
    grad_wv[...] = whole_b(2)


def rope_table(count):
    half_head = HEAD_SIZE // 2
    frequencies = np.power(
        np.float32(rope_base), np.float32(-2.0) * np.arange(half_head, dtype=np.float32) / HEAD_SIZE
    ).astype(np.float32)
    angles = np.arange(count, dtype=np.float32)[:, None] * frequencies[None, :]
    return np.concatenate([np.cos(angles), np.sin(angles)], axis=1).astype(np.float32)


def hand_on_kernel(*refs):
    count = len(refs) // 2
    for i in range(count):
        refs[count + i][...] = refs[i][...]


def shards(
    x_prompt,
    x_comp,
    up_prompt,
    up_comp,
    w_q,
    key_projection,
    value_projection,
    w_o,
    pre_gain,
    post_gain,
    dpo_weight,
    prompt_len,
    comp_len,
    loss_mask,
):
    rows_p, rows_c, width = x_prompt.shape[1], x_comp.shape[2], x_prompt.shape[2]
    half, comp = 8 * rows_p, 8 * rows_c
    rope = jnp.asarray(rope_table(2 * half + comp))
    bf, f32 = jnp.bfloat16, jnp.float32
    vm, anywhere, smem = (
        pl.BlockSpec(memory_space=pltpu.VMEM),
        pl.BlockSpec(memory_space=pl.ANY),
        pl.BlockSpec(memory_space=pltpu.SMEM),
    )
    dma = pltpu.SemaphoreType.DMA
    out = pl.pallas_call(
        block_kernel,
        out_shape=(
            jax.ShapeDtypeStruct((rows_p, width), bf),
            jax.ShapeDtypeStruct((rows_c, width), bf),
            jax.ShapeDtypeStruct((144, 256), f32),
            jax.ShapeDtypeStruct((144, 128), f32),
            jax.ShapeDtypeStruct((144, 128), f32),
            jax.ShapeDtypeStruct((144, 256), f32),
        ),
        in_specs=[anywhere] * 8 + [vm] * 2 + [anywhere] + [smem] * 4,
        out_specs=[vm] * 6,
        scratch_shapes=[
            pltpu.VMEM((half, 128), f32),
            pltpu.VMEM((half, 128), f32),
            pltpu.VMEM((comp, 128), f32),
            pltpu.VMEM((comp, 128), f32),
            pltpu.VMEM((2 * half + comp, 128), f32),
            pltpu.VMEM((rows_p, width), bf),
            pltpu.VMEM((rows_c, width), bf),
            pltpu.VMEM((rows_p, width), bf),
            pltpu.VMEM((rows_c, width), bf),
            pltpu.VMEM((width, 512), bf),
            pltpu.VMEM((256, width), bf),
            pltpu.VMEM((8, rows_p, width), bf),
            pltpu.VMEM((8, rows_c, width), bf),
            pltpu.VMEM((8, rows_p, width), bf),
            pltpu.VMEM((8, rows_c, width), bf),
            pltpu.VMEM((3 * STEPS, rows_p, PIECE), bf),
            pltpu.VMEM((3 * STEPS, rows_c, PIECE), bf),
            pltpu.VMEM((8, rows_p, width), bf),
            pltpu.VMEM((8, rows_c, width), bf),
            pltpu.VMEM((half + comp, 256), bf),
            pltpu.VMEM((2 * half + comp, 256), bf),
            pltpu.VMEM((half + comp, 256), bf),
            pltpu.VMEM((2, half, 2 * half), f32),
            pltpu.VMEM((2, comp, 2 * half + comp), f32),
            pltpu.VMEM((2, half, 2 * half), f32),
            pltpu.VMEM((2, comp, 2 * half + comp), f32),
            pltpu.VMEM((2 * half, 256), f32),
            pltpu.VMEM((half, 256), bf),
            pltpu.VMEM((half, 256), bf),
            pltpu.VMEM((half + comp, 256), bf),
            pltpu.VMEM((half + comp, 256), bf),
            pltpu.VMEM((3, 2, 2, 8, 2, 144, 128), bf),
            pltpu.VMEM((3, 2, 2, 8, 144, 128), bf),
            pltpu.VMEM((3, 2, 144, 128), bf),
            pltpu.VMEM((3, 2, 3, 2, 144, 128), bf),
            pltpu.VMEM((3, 80, 128), bf),
            pltpu.VMEM((3, 64, 128), bf),
            pltpu.VMEM((3, 2, 3, 144, 128), bf),
            pltpu.VMEM((3, 144, 128), bf),
            pltpu.VMEM((3, 144, 128), bf),
            pltpu.VMEM((3, 8, 144, 128), bf),
            pltpu.VMEM((3, 8, 144, 128), bf),
            dma((9,)),
            dma((6,)),
            dma((18 * STEPS,)),
            dma((2,)),
            dma((2,)),
            dma((12,)),
            dma((12,)),
            dma((48,)),
            dma((48,)),
            dma((3,)),
            dma((3,)),
            dma((6,)),
            dma((6,)),
        ],
        compiler_params=pltpu.CompilerParams(
            collective_id=1, has_side_effects=True, vmem_limit_bytes=60 << 20
        ),
        name="block",
    )(
        x_prompt[0], x_comp[0, 0], up_prompt[0], up_comp[0, 0],
        w_q, key_projection, value_projection, w_o,
        pre_gain, post_gain, rope,
        dpo_weight, prompt_len, comp_len, loss_mask[0, 0],
    )
    out_p, out_c, grad_wq, grad_wk, grad_wv, grad_wo = pl.pallas_call(
        hand_on_kernel,
        out_shape=tuple(jax.ShapeDtypeStruct(o.shape, o.dtype) for o in out),
        in_specs=[vm] * 6,
        out_specs=[vm] * 6,
        name="hand_on",
    )(*out)
    return (out_p[None], out_c[None, None], grad_wq, grad_wk, grad_wv, grad_wo.T)


def solution(mesh):
    in_specs = (
        P("dp", ("pair", "tp"), None),
        P("dp", "pair", "tp", None),
        P("dp", ("pair", "tp"), None),
        P("dp", "pair", "tp", None),
        P(None, "tp"),
        P(None, "tp"),
        P(None, "tp"),
        P("tp", None),
        P(),
        P(),
        P("dp"),
        P("dp"),
        P("dp", "pair"),
        P("dp", "pair", None),
    )
    out_specs = (
        P("dp", ("pair", "tp"), None),
        P("dp", "pair", "tp", None),
        P(("pair", "dp"), "tp"),
        P(("pair", "dp"), "tp"),
        P(("pair", "dp"), "tp"),
        P("tp", ("pair", "dp")),
    )
    return jax.shard_map(shards, mesh=mesh, in_specs=in_specs, out_specs=out_specs, check_vma=False)
```

profile of v0, /device:TPU:2, one launch (start us, length us, event | category | flops | bytes accessed | tf_op | source)
XLA Modules:
  0.0 141.5 jit_solution(5194921988664282472)
XLA Ops:
  2.6 136.8 %block.1 = (bf16[32,4608]{1,0:T(8,128)(2,1)}, bf16[16,4608]{1,0:T(8,128)(2,1)}, f32[144,256]{1,0:T(8,128)}, f32[144,128]{1,0:T(8,128)}, f32[144,128]{1,0:T(8,128)}, /*index=5*/f32[144,256]{1,0:T(8,128)}) custom-call(bf16[32,4608]{1,0:T(8,128)(2,1)} %bitcast.8, bf16[16,4608]{1,0:T(8,128)(2,1)} %bitcast.10, bf16[32,4608]{1,0:T(8,128)(2,1)} %bitcast.9, ...), custom_call_target="tpu_custom_call" | custom-call | tf_op jit(solution)/shard_map/block/pallas_call | solution.py:799
  139.4 2.1 %hand_on.1 = (bf16[32,4608]{1,0:T(8,128)(2,1)}, bf16[16,4608]{1,0:T(8,128)(2,1)}, f32[144,256]{1,0:T(8,128)}, f32[144,128]{1,0:T(8,128)}, f32[144,128]{1,0:T(8,128)}, /*index=5*/f32[144,256]{1,0:T(8,128)}) custom-call(bf16[32,4608]{1,0:T(8,128)(2,1)} %get-tuple-element.18.refs_0_, bf16[16,4608]{1,0:T(8,128)(2,1)} %get-tuple-element.19.refs_1_, ...), custom_call_target="tpu_custom_call" | custom-call | tf_op jit(solution)/shard_map/hand_on/pallas_call | solution.py:878
where the time goes:
time: 142 us
  Pallas kernels  139 us (98%)
  between operations  2.58 us (2%)
    pallas_call x1, Pallas kernels, shards(): pl.pallas_call(block_kernel, out_shape=(jax.ShapeDtypeStruct((rows_p, wid...  137 us

commit v1 on v0

--- a/solution.py
+++ b/solution.py
@@ -286,9 +286,9 @@
     out_p, out_c, grad_wq, grad_wk, grad_wv, grad_wo,
     cos_p, sin_p, cos_c, sin_c, table, xp, xc, upp, upc, wqkv, wo, nbp, nbc, brp, brc, gotp, gotc, gbp, gbc,
     qs, kv, att, prob_p, prob_c, damp_p, damp_c, dkv, dkv_out, dkv_in, gq, gkv,
-    wg, core_in, a_half, a_full, b_up, b_down, b_full, pair_out, pair_in, cross_out, cross_in,
+    wg, core_in, a_half, a_full, b_up, b_down, b_full, pair_out, pair_in, cross_out, cross_in, done_p, done_c,
     load_sems, tp_send, tp_recv, kv_send, kv_recv, core_send, core_recv,
-    z_send, z_recv, pair_send, pair_recv, cross_send, cross_recv,
+    z_send, z_recv, pair_send, pair_recv, cross_send, cross_recv, store_sems,
 ):
     side = lax.axis_index("pair")
     me = lax.axis_index("tp")
@@ -313,8 +313,8 @@
             ]
         )
     ]
-    for load in loads:
-        load.start()
+    loads[0].start()
+    loads[1].start()
     barrier = pltpu.get_barrier_semaphore()
     peers = [stream_target(s) for s in range(3)] + [partner, other_core, z_up, z_down]
     for peer in peers:
@@ -345,6 +345,8 @@
     nbp[me] = normalize(xp)
     pl.semaphore_wait(barrier, len(peers))
     gather_p.start()
+    for load in loads[2:]:
+        load.start()
     loads[1].wait()
     nbc[me] = normalize(xc)
     for t in range(STEPS):
@@ -457,20 +459,26 @@
     loads[6].wait()
     loads[7].wait()
     token = side * half + me * rows_p + iota((rows_p, 1), 0)
-    out_p[...], gbp[me] = finish_branch(xp, upp, brp[me], (token < length).astype(jnp.float32))
+    done_p[...], gbp[me] = finish_branch(xp, upp, brp[me], (token < length).astype(jnp.float32))
     regather_p.start()
-    ticker.add(steps_of(reduce_c))
-    ticker.drain()
+    store_p = pltpu.make_async_copy(done_p, out_p, store_sems.at[0])
+    store_p.start()
+    for t in range(STEPS):
+        reduce_c.step(t)
+        if t >= 8:
+            regather_p.step(t - 8)
     slot = iota((rows_c, 1), 0)
     keep = jnp.zeros((rows_c, 1), jnp.float32)
     for i in range(rows_c):
         keep = jnp.where(slot == i, loss_mask[me * rows_c + i].astype(jnp.float32), keep)
     direction = 1.0 - 2.0 * side.astype(jnp.float32)
     real = (me * rows_c + slot < comp_len[0, 0]).astype(jnp.float32)
-    out_c[...], gbc[me] = finish_branch(
+    done_c[...], gbc[me] = finish_branch(
         xc, upc, brc[me], dpo_weight[0] * direction * keep * real
     )
-    for t in range(STEPS):
+    store_c = pltpu.make_async_copy(done_c, out_c, store_sems.at[1])
+    store_c.start()
+    for t in range(STEPS - 8, STEPS):
         regather_p.step(t)
         if t == 10:
             regather_c.start()
@@ -732,6 +740,8 @@
     z_step(2, 0, 1)
     z_step(1, 1, 1)
     z_step(2, 1, 0)
+    store_p.wait()
+    store_c.wait()
     kv_copy.wait_send()
     regather_p.finish_sends()
     regather_c.finish_sends()
@@ -807,7 +817,7 @@
             jax.ShapeDtypeStruct((144, 256), f32),
         ),
         in_specs=[anywhere] * 8 + [vm] * 2 + [anywhere] + [smem] * 4,
-        out_specs=[vm] * 6,
+        out_specs=[anywhere] * 2 + [vm] * 4,
         scratch_shapes=[
             pltpu.VMEM((half, 128), f32),
             pltpu.VMEM((half, 128), f32),
@@ -851,6 +861,8 @@
             pltpu.VMEM((3, 144, 128), bf),
             pltpu.VMEM((3, 8, 144, 128), bf),
             pltpu.VMEM((3, 8, 144, 128), bf),
+            pltpu.VMEM((rows_p, width), bf),
+            pltpu.VMEM((rows_c, width), bf),
             dma((9,)),
             dma((6,)),
             dma((18 * STEPS,)),
@@ -864,6 +876,7 @@
             dma((3,)),
             dma((6,)),
             dma((6,)),
+            dma((2,)),
         ],
         compiler_params=pltpu.CompilerParams(
             collective_id=1, has_side_effects=True, vmem_limit_bytes=60 << 20

time: 142 us -> 139 us (0.979)
  Pallas kernels: 139 us -> 136 us
    pallas_call x1, Pallas kernels: 137 us -> 134 us  [shards(): pl.pallas_call(block_kernel, out_shape=(jax.ShapeDtypeStruct((rows_p, wid...]
where the time goes in v1:
time: 139 us; the launch traced here: 138 us
  Pallas kernels  136 us (98%)
  between operations  2.58 us (2%)
    pallas_call x1, Pallas kernels, shards(): pl.pallas_call(block_kernel, out_shape=(jax.ShapeDtypeStruct((rows_p, wid...  134 us

profile of v1, /device:TPU:2, one launch (start us, length us, event | category | flops | bytes accessed | tf_op | source)
XLA Modules:
  0.0 138.5 jit_solution(3727419582580464425)
XLA Ops:
  2.6 133.8 %block.1 = (bf16[32,4608]{1,0:T(8,128)(2,1)}, bf16[16,4608]{1,0:T(8,128)(2,1)}, f32[144,256]{1,0:T(8,128)}, f32[144,128]{1,0:T(8,128)}, f32[144,128]{1,0:T(8,128)}, /*index=5*/f32[144,256]{1,0:T(8,128)}) custom-call(bf16[32,4608]{1,0:T(8,128)(2,1)} %bitcast.8, bf16[16,4608]{1,0:T(8,128)(2,1)} %bitcast.10, bf16[32,4608]{1,0:T(8,128)(2,1)} %bitcast.9, ...), custom_call_target="tpu_custom_call" | custom-call | tf_op jit(solution)/shard_map/block/pallas_call | solution.py:809
  136.3 2.1 %hand_on.1 = (bf16[32,4608]{1,0:T(8,128)(2,1)}, bf16[16,4608]{1,0:T(8,128)(2,1)}, f32[144,256]{1,0:T(8,128)}, f32[144,128]{1,0:T(8,128)}, f32[144,128]{1,0:T(8,128)}, /*index=5*/f32[144,256]{1,0:T(8,128)}) custom-call(bf16[32,4608]{1,0:T(8,128)(2,1)} %get-tuple-element.18.refs_0_, bf16[16,4608]{1,0:T(8,128)(2,1)} %get-tuple-element.19.refs_1_, ...), custom_call_target="tpu_custom_call" | custom-call | tf_op jit(solution)/shard_map/hand_on/pallas_call | solution.py:891
